TPU v7x, 256 devices: a whole 4x4x8 slice. The times are simulated.
256 devices in a mesh: wide: 128 (over x, z, y_lo, core), narrow: 2 (over y_hi).
Axes of the slice: x: 4, y: 4 (y_hi: 2, y_lo: 2; y = y_hi * 2 + y_lo), z: 8, core: 2. Of those that a mesh axis runs over, the one named last changes fastest.
Arguments:
- frames: bfloat16 [131072, 768], P(('wide', 'narrow')), may hold values from -6 to 6
- down_kernel: bfloat16 [15, 768], replicated, may hold values from -1.5 to 1.5
- proj_weight: bfloat16 [768, 1024], P('wide'), may hold values from -0.21875 to 0.21875
- glu_weight: bfloat16 [1024, 2, 1024], P('wide', None, 'narrow'), may hold values from -0.1875 to 0.1875
- conv_kernel: bfloat16 [15, 1024], P(None, 'narrow'), may hold values from -1.5 to 1.5
- conv_out_weight: bfloat16 [1024, 1024], P('narrow', 'wide'), may hold values from -0.5 to 0.5
- ffn_in: bfloat16 [1024, 4096], P('wide', 'narrow'), may hold values from -0.1875 to 0.1875
- ffn_out: bfloat16 [4096, 1024], P('narrow', 'wide'), may hold values from -0.25 to 0.25
Outputs:
- section_out: bfloat16 [65536, 1024], P(('wide', 'narrow'))
All inputs are finite; a program needn't handle non-finite values.
Results may differ from a plain program's by a relative error of at most 0.017.
Values may be sent and summed in bfloat16 or wider, within the bound.
No kernel may reach another device: no remote copies, remote signals or barrier semaphores. Data moves between devices by JAX's collectives and lax.ppermute only.
A program may use at most 64 MiB of HBM per device.

v0:
```python
import jax
import jax.numpy as jnp
from jax import lax
from jax.sharding import PartitionSpec as P


def padded_2(x, sides, width):
    for axis, dim in sides:
        peers, length = (lax.axis_size(axis), x.shape[dim])
        up = [(i, (i + 1) % peers) for i in range(peers - 1)]
        down = [(j, i) for i, j in up]
        last = lax.slice_in_dim(x, length - width, length, axis=dim)
        leading = lax.slice_in_dim(x, 0, width, axis=dim)
        before = lax.ppermute(last, axis, up)
        after = lax.ppermute(leading, axis, down)
        x = jnp.concatenate([before, x, after], axis=dim)
    return x


def layer_norm(values):
    centre = jnp.mean(values, axis=-1, keepdims=True)
    centred = values - centre
    spread = jnp.mean(centred * centred, axis=-1, keepdims=True)
    return centred * lax.rsqrt(spread + 1e-05)


def body(
    frames, down_kernel, proj_weight, glu_weight, conv_kernel, conv_out_weight, ffn_in, ffn_out
):
    taps = down_kernel.shape[0]
    reach = taps // 2
    frame_rows = frames.shape[0]
    channels = frames.shape[1]
    padded = padded_2(frames, ((("wide", "narrow"), 0),), reach)
    padded_wide = padded.astype(jnp.float32)
    down_taps = down_kernel.astype(jnp.float32)
    reduced = jnp.zeros((frame_rows // 2, channels), jnp.float32)
    for offset in range(taps):
        window = lax.slice(padded_wide, (offset, 0), (offset + frame_rows - 1, channels), (2, 1))
        reduced = reduced + down_taps[offset] * window
    reduced = reduced.astype(jnp.bfloat16)
    source = lax.all_gather(reduced, "narrow", axis=0, tiled=True)
    empty = jnp.zeros((source.shape[0], proj_weight.shape[1]), jnp.float32)
    shard_piece = lax.all_gather(proj_weight, "wide", axis=0, tiled=True)
    columns = lax.slice_in_dim(source, 0, shard_piece.shape[0], axis=1)
    summed = empty + jnp.dot(columns, shard_piece, preferred_element_type=jnp.float32)
    projected = summed.astype(jnp.bfloat16)
    block_rows = projected.shape[0]
    normed = layer_norm(projected.astype(jnp.float32)).astype(jnp.bfloat16)
    glu_empty = jnp.zeros((block_rows, 2, glu_weight.shape[2]), jnp.float32)
    shard_piece = lax.all_gather(glu_weight, "wide", axis=0, tiled=True)
    columns = lax.slice_in_dim(normed, 0, shard_piece.shape[0], axis=1)
    glu_pre = glu_empty + jnp.einsum(
        "rc,cgh->rgh", columns, shard_piece, preferred_element_type=jnp.float32
    )
    gated = (glu_pre[:, 0, :] * jax.nn.sigmoid(glu_pre[:, 1, :])).astype(jnp.bfloat16)
    gated_pad = padded_2(gated, (("wide", 0),), reach).astype(jnp.float32)
    conv_taps = conv_kernel.astype(jnp.float32)
    depth = jnp.zeros(gated.shape, jnp.float32)
    for offset in range(taps):
        depth = depth + conv_taps[offset] * gated_pad[offset : offset + block_rows]
    activated = jax.nn.silu(depth).astype(jnp.bfloat16)
    conv_part = jnp.dot(
        activated,
        lax.all_gather(conv_out_weight, "wide", axis=1, tiled=True),
        preferred_element_type=jnp.float32,
    )
    half_rows = block_rows // 2
    own_start = lax.axis_index("narrow") * half_rows
    mixed = projected.astype(jnp.float32) + lax.psum(
        conv_part.astype(jnp.bfloat16), "narrow"
    ).astype(jnp.float32)
    own_mixed = lax.dynamic_slice_in_dim(mixed, own_start, half_rows, 0)
    second_norm = layer_norm(mixed).astype(jnp.bfloat16)
    ffn_empty = jnp.zeros((block_rows, ffn_in.shape[1]), jnp.float32)
    shard_piece = lax.all_gather(ffn_in, "wide", axis=0, tiled=True)
    columns = lax.slice_in_dim(second_norm, 0, shard_piece.shape[0], axis=1)
    hidden_pre = ffn_empty + jnp.dot(columns, shard_piece, preferred_element_type=jnp.float32)
    hidden = jax.nn.silu(hidden_pre).astype(jnp.bfloat16)
    ffn_part = jnp.dot(
        hidden,
        lax.all_gather(ffn_out, "wide", axis=1, tiled=True),
        preferred_element_type=jnp.float32,
    )
    ffn_share = lax.psum_scatter(
        ffn_part.astype(jnp.bfloat16), "narrow", scatter_dimension=0, tiled=True
    ).astype(jnp.float32)
    return (own_mixed + 0.5 * ffn_share).astype(jnp.bfloat16)


def solution(mesh):
    return jax.shard_map(
        body,
        mesh=mesh,
        in_specs=(
            P(("wide", "narrow"), None),
            P(),
            P("wide", None),
            P("wide", None, "narrow"),
            P(None, "narrow"),
            P("narrow", "wide"),
            P("wide", "narrow"),
            P("narrow", "wide"),
        ),
        out_specs=P(("wide", "narrow"), None),
        check_vma=False,
    )
```

profile of v0, /device:TPU:1, one launch (start us, length us, event | category | flops | bytes accessed | tf_op | source)
XLA Modules:
  0.0 1187.8 jit_solution(15642934463695296659)
XLA Ops:
  6.5 0.0 all-gather.15.cloned.1.call-start
  6.5 0.7 all-gather.15.cloned.1.call-update
  7.3 0.0 all-gather.7.cloned.1.call-start
  7.3 1.3 copy.11
  8.6 0.0 all-gather.7.cloned.1.call-update
  8.7 0.0 all-gather.9.cloned.1.call-start
  8.7 0.7 fusion.38
  9.4 5.6 collective-permute-start
  15.1 2.5 collective-permute-start.1
  17.6 0.0 all-gather.9.cloned.1.call-update
  17.6 0.0 all-reduce.2.cloned.1.call-start
  17.6 0.7 convert_element_type.52
  18.4 1.0 fusion.39
  19.4 0.1 slice_reduce_fusion.14
  19.6 0.0 collective-permute-done
  19.6 1.5 collective-permute-done.1
  21.0 1.3 maximum_convert_fusion
  22.3 0.7 slice.201
  23.0 0.7 slice.203
  23.7 2.8 slice.205
  26.5 2.8 slice.207
  29.3 2.8 slice.209
  32.2 2.8 slice.211
  35.0 2.8 slice.213
  37.8 2.8 slice.215
  40.5 2.7 slice.217
  43.3 2.8 slice.219
  46.1 2.8 slice.221
  48.9 2.8 slice.223
  51.7 2.8 slice.225
  54.5 2.8 slice.227
  57.3 2.8 slice.229
  60.1 4.8 add_convert_fusion.1
  64.9 10.7 all_gather.18
  75.6 149.7 %all-gather.15.cloned.1.call-done = bf16[128,6,1024]{2,1,0:T(8,128)(2,1)} async-done(((bf16[1,6,1024]{2,1,0:T(8,128)(2,1)}), bf16[128,6,1024]{2,1,0:T(8,128)(2,1)}) %all-gather.15.cloned.1.call-update) | async-done | bytes 1572880 | tf_op jit(solution)/shard_map/all_gather | solution.py:44
  225.3 2.6 reshape.35
  227.9 1.1 convert_reduce_fusion
  229.0 0.4 fusion.2
  229.4 210.3 %all-gather.7.cloned.1.call-done = bf16[1024,2,512]{2,0,1:T(8,128)(2,1)} async-done(((bf16[8,2,512]{2,0,1:T(8,128)(2,1)}), bf16[1024,2,512]{2,0,1:T(8,128)(2,1)}) %all-gather.7.cloned.1.call-update) | async-done | bytes 2097168 | tf_op jit(solution)/shard_map/all_gather | solution.py:51
  439.8 2.9 fusion.8
  442.7 0.3 fusion.34
  443.0 2.5 collective-permute-start.2
  445.4 1.9 collective-permute-start.3
  447.4 0.3 fusion.46
  447.6 0.0 collective-permute-done.2
  447.7 2.7 collective-permute-done.3
  450.4 0.1 maximum_convert_fusion.1
  450.6 200.3 %all-gather.9.cloned.1.call-done = bf16[512,1024]{0,1:T(8,128)(2,1)} async-done(((bf16[512,8]{0,1:T(8,128)(2,1)}), bf16[512,1024]{0,1:T(8,128)(2,1)}) %all-gather.9.cloned.1.call-update) | async-done | bytes 1048592 | tf_op jit(solution)/shard_map/all_gather | solution.py:65
  650.8 4.7 convolution_convert_fusion.1
  655.6 0.0 all-reduce.2.cloned.1.call-update
  655.6 0.0 all-gather.11.cloned.1.call-start
  655.6 0.5 all-gather.11.cloned.1.call-update
  656.2 0.0 all-gather.13.cloned.1.call-start
  656.2 0.5 all-gather.13.cloned.1.call-update
  656.8 0.2 reduce-scatter.2.cloned.1.call-start
  657.0 52.1 %all-reduce.2.cloned.1.call-done = bf16[512,1024]{1,0:T(8,128)(2,1)} async-done(((bf16[512,1024]{1,0:T(8,128)(2,1)}), bf16[512,1024]{1,0:T(8,128)(2,1)}) %all-reduce.2.cloned.1.call-update) | async-done | bytes 1048592 | tf_op jit(solution)/shard_map/psum | solution.py:70
  709.1 1.7 convert_add_fusion
  710.8 0.5 multiply_reduce_fusion
  711.3 214.3 %all-gather.11.cloned.1.call-done = bf16[1024,2048]{1,0:T(8,128)(2,1)} async-done(((bf16[8,2048]{1,0:T(8,128)(2,1)}), bf16[1024,2048]{1,0:T(8,128)(2,1)}) %all-gather.11.cloned.1.call-update) | async-done | bytes 4194320 | tf_op jit(solution)/shard_map/all_gather | solution.py:76
  925.6 216.9 %all-gather.13.cloned.1.call-done = bf16[2048,1024]{0,1:T(8,128)(2,1)} async-done(((bf16[2048,8]{0,1:T(8,128)(2,1)}), bf16[2048,1024]{0,1:T(8,128)(2,1)}) %all-gather.13.cloned.1.call-update) | async-done | bytes 4194320 | tf_op jit(solution)/shard_map/all_gather | solution.py:82
  1142.5 9.5 fusion.5
  1152.1 0.0 reduce-scatter.2.cloned.1.call-update
  1152.1 26.9 %reduce-scatter.2.cloned.1.call-done = bf16[256,1024]{1,0:T(8,128)(2,1)} async-done(((bf16[512,1024]{1,0:T(8,128)(2,1)}), bf16[256,1024]{1,0:T(8,128)(2,1)}) %reduce-scatter.2.cloned.1.call-update) | async-done | bytes 524304 | tf_op jit(solution)/shard_map/reduce_scatter | solution.py:85
  1179.0 2.0 add_convert_fusion
  (7 shorter events, 0.0 us)
Async XLA Ops:
  6.5 218.8 %all-gather.15.cloned.1.call-start = ((), (), s32[]{:S(2)}) async-start(), calls=%async_computation.7 | async-start | bytes 2113536 | tf_op jit(solution)/shard_map/all_gather | solution.py:44
  7.3 432.5 %all-gather.7.cloned.1.call-start = ((), (), s32[]{:S(2)}) async-start(), calls=%async_computation.1 | async-start | bytes 2113536 | tf_op jit(solution)/shard_map/all_gather | solution.py:51
  8.7 642.2 %all-gather.9.cloned.1.call-start = ((), (), s32[]{:S(2)}) async-start(), calls=%async_computation.2 | async-start | bytes 1056768 | tf_op jit(solution)/shard_map/all_gather | solution.py:65
  9.4 10.1 collective-permute-start
  15.1 5.9 collective-permute-start.1
  17.6 691.5 %all-reduce.2.cloned.1.call-start = ((), (), s32[]{:S(2)}) async-start(), calls=%async_computation.3 | async-start | bytes 2097152 | tf_op jit(solution)/shard_map/psum | solution.py:70
  443.0 4.7 collective-permute-start.2
  445.4 5.0 collective-permute-start.3
  655.6 270.0 %all-gather.11.cloned.1.call-start = ((), (), s32[]{:S(2)}) async-start(), calls=%async_computation.4 | async-start | bytes 4227072 | tf_op jit(solution)/shard_map/all_gather | solution.py:76
  656.2 486.3 %all-gather.13.cloned.1.call-start = ((), (), s32[]{:S(2)}) async-start(), calls=%async_computation.5 | async-start | bytes 4227072 | tf_op jit(solution)/shard_map/all_gather | solution.py:82
  656.8 522.2 %reduce-scatter.2.cloned.1.call-start = ((), (), s32[]{:S(2)}) async-start(), calls=%async_computation.6 | async-start | bytes 1572864 | tf_op jit(solution)/shard_map/reduce_scatter | solution.py:85
  709.1 1.7 copy-start
Sparse Core Ops, SparseCore 0:
  9.2 216.0 all-gather.14
  227.2 212.4 all-gather.6
  441.6 209.1 all-gather.8
  655.7 53.3 all-reduce.1
  711.0 214.6 all-gather.10
  927.5 214.9 all-gather.12
  1152.2 26.7 reduce-scatter.1
where the time goes:
time: 1190 us
  waiting for transfers between devices  1080 us (91%)
  local copies, waits for them, and re-layouts  43.6 us (4%)
  matrix products  18.2 us (2%)
  between operations  13.6 us (1%)
  starting transfers between devices  12.9 us (1%)
  other arithmetic  12.2 us (1%)
    all_gather x1, waiting for transfers between devices, body(): lax.all_gather(ffn_out, 'wide', axis=1, tiled=True)  217 us
    all_gather x1, waiting for transfers between devices, body(): shard_piece = lax.all_gather(ffn_in, 'wide', axis=0, tiled=True)  214 us
    all_gather x1, waiting for transfers between devices, body(): shard_piece = lax.all_gather(glu_weight, 'wide', axis=0, tiled=True)  210 us
    all_gather x1, waiting for transfers between devices, body(): lax.all_gather(conv_out_weight, 'wide', axis=1, tiled=True)  200 us
    all_gather x1, waiting for transfers between devices, body(): shard_piece = lax.all_gather(proj_weight, 'wide', axis=0, tiled=True)  150 us
    psum x1, waiting for transfers between devices, body(): lax.psum(conv_part.astype(jnp.bfloat16), 'narrow').astype(jnp.float32)  52.1 us
    slice x15, local copies, waits for them, and re-layouts, body(): lax.slice(padded_wide, (offset, 0), (offset + frame_rows - 1, channels),...  37.8 us
    reduce_scatter x1, waiting for transfers between devices, body(): lax.psum_scatter(ffn_part.astype(jnp.bfloat16), 'narrow', scatter_dimensi...  26.9 us
  transfers between devices with their start and end apart: 11, of which 9 were waited for; matrix products, arithmetic and copies ran while one was open for 5% of the time, Pallas kernels for 0%

commit v1 on v0

--- a/solution.py
+++ b/solution.py
@@ -73,7 +73,9 @@
     own_mixed = lax.dynamic_slice_in_dim(mixed, own_start, half_rows, 0)
     second_norm = layer_norm(mixed).astype(jnp.bfloat16)
     ffn_empty = jnp.zeros((block_rows, ffn_in.shape[1]), jnp.float32)
-    shard_piece = lax.all_gather(ffn_in, "wide", axis=0, tiled=True)
+    shard_piece = jnp.concatenate(
+        lax.all_to_all(jnp.stack([ffn_in] * lax.axis_size("wide")), "wide", 0, 0), axis=0
+    )
     columns = lax.slice_in_dim(second_norm, 0, shard_piece.shape[0], axis=1)
     hidden_pre = ffn_empty + jnp.dot(columns, shard_piece, preferred_element_type=jnp.float32)
     hidden = jax.nn.silu(hidden_pre).astype(jnp.bfloat16)

time: 1190 us -> 1000 us (0.84)
  waiting for transfers between devices: 1080 us -> 877 us
    all_gather x1 -> x0, waiting for transfers between devices: 214 us -> none  [body(): shard_piece = lax.all_gather(ffn_in, 'wide', axis=0, tiled=True)]
    all_gather x1, waiting for transfers between devices: 217 us -> 193 us  [body(): lax.all_gather(ffn_out, 'wide', axis=1, tiled=True)]
    all_to_all x0 -> x1, waiting for transfers between devices: none -> 22.3 us  [body(): lax.all_to_all(jnp.stack([ffn_in] * lax.axis_size('wide')), 'wide', 0, 0)]
    psum x1, waiting for transfers between devices: 52.1 us -> 68.7 us  [body(): lax.psum(conv_part.astype(jnp.bfloat16), 'narrow').astype(jnp.float32)]
  transfers between devices with their start and end apart: 11 -> 11, of which waited for: 9 -> 9; matrix products, arithmetic and copies ran while one was open for 5% -> 6% of each run, Pallas kernels for 0% -> 0%
where the time goes in v1:
time: 1000 us
  waiting for transfers between devices  877 us (88%)
  local copies, waits for them, and re-layouts  46.1 us (5%)
  starting transfers between devices  23.6 us (2%)
  matrix products  18.3 us (2%)
  between operations  13.6 us (1%)
  other arithmetic  12.2 us (1%)
  blocking collectives  10.7 us (1%)
    all_gather x1, waiting for transfers between devices, body(): shard_piece = lax.all_gather(glu_weight, 'wide', axis=0, tiled=True)  210 us
    all_gather x1, waiting for transfers between devices, body(): lax.all_gather(conv_out_weight, 'wide', axis=1, tiled=True)  200 us
    all_gather x1, waiting for transfers between devices, body(): lax.all_gather(ffn_out, 'wide', axis=1, tiled=True)  193 us
    all_gather x1, waiting for transfers between devices, body(): shard_piece = lax.all_gather(proj_weight, 'wide', axis=0, tiled=True)  150 us
    psum x1, waiting for transfers between devices, body(): lax.psum(conv_part.astype(jnp.bfloat16), 'narrow').astype(jnp.float32)  68.7 us
    slice x15, local copies, waits for them, and re-layouts, body(): lax.slice(padded_wide, (offset, 0), (offset + frame_rows - 1, channels),...  37.8 us
    reduce_scatter x1, waiting for transfers between devices, body(): lax.psum_scatter(ffn_part.astype(jnp.bfloat16), 'narrow', scatter_dimensi...  27.4 us
    all_to_all x1, waiting for transfers between devices, body(): lax.all_to_all(jnp.stack([ffn_in] * lax.axis_size('wide')), 'wide', 0, 0)  22.3 us
  transfers between devices with their start and end apart: 11, of which 9 were waited for; matrix products, arithmetic and copies ran while one was open for 6% of the time, Pallas kernels for 0%

profile of v1, /device:TPU:1, one launch (start us, length us, event | category | flops | bytes accessed | tf_op | source)
XLA Modules:
  0.0 1002.0 jit_solution(5685846175813376551)
XLA Ops:
  6.5 0.0 all-gather.12.cloned.1.call-start
  6.5 0.7 all-gather.12.cloned.1.call-update
  7.3 0.0 all-gather.6.cloned.1.call-start
  7.3 1.3 copy.11
  8.6 0.0 all-gather.6.cloned.1.call-update
  8.7 0.0 all-gather.8.cloned.1.call-start
  8.7 0.7 fusion.45
  9.4 5.6 collective-permute-start
  15.1 2.5 collective-permute-start.1
  17.6 0.0 all-gather.8.cloned.1.call-update
  17.6 0.0 all-reduce.2.cloned.1.call-start
  17.6 0.7 convert_element_type.52
  18.4 1.0 fusion.46
  19.4 0.1 slice_reduce_fusion.14
  19.6 0.0 collective-permute-done
  19.6 1.5 collective-permute-done.1
  21.0 1.3 maximum_convert_fusion
  22.3 0.7 slice.201
  23.0 0.7 slice.203
  23.7 2.8 slice.205
  26.5 2.8 slice.207
  29.3 2.8 slice.209
  32.2 2.8 slice.211
  35.0 2.8 slice.213
  37.8 2.8 slice.215
  40.5 2.7 slice.217
  43.3 2.8 slice.219
  46.1 2.8 slice.221
  48.9 2.8 slice.223
  51.7 2.8 slice.225
  54.5 2.8 slice.227
  57.3 2.8 slice.229
  60.1 4.8 add_convert_fusion.1
  64.9 10.7 %all_gather.15 = bf16[512,768]{1,0:T(8,128)(2,1)S(1)} all-gather(bf16[256,768]{1,0:T(8,128)(2,1)S(1)} %add_convert_fusion.1), channel_id=1, replica_groups=mesh['wide'=128,'narrow'=2] {'narrow'}, dimensions={0}, use_global_device_ids=true | all-gather | bytes 1179648 | tf_op jit(solution)/shard_map/all_gather | solution.py:42
  75.6 149.7 %all-gather.12.cloned.1.call-done = bf16[128,6,1024]{2,1,0:T(8,128)(2,1)} async-done(((bf16[1,6,1024]{2,1,0:T(8,128)(2,1)}), bf16[128,6,1024]{2,1,0:T(8,128)(2,1)}) %all-gather.12.cloned.1.call-update) | async-done | bytes 1572880 | tf_op jit(solution)/shard_map/all_gather | solution.py:44
  225.3 2.6 reshape.41
  227.9 1.1 convert_reduce_fusion
  229.0 0.4 fusion.4
  229.4 210.3 %all-gather.6.cloned.1.call-done = bf16[1024,2,512]{2,0,1:T(8,128)(2,1)} async-done(((bf16[8,2,512]{2,0,1:T(8,128)(2,1)}), bf16[1024,2,512]{2,0,1:T(8,128)(2,1)}) %all-gather.6.cloned.1.call-update) | async-done | bytes 2097168 | tf_op jit(solution)/shard_map/all_gather | solution.py:51
  439.8 2.9 fusion.15
  442.7 0.3 fusion.41
  443.0 2.5 collective-permute-start.2
  445.4 1.9 collective-permute-start.3
  447.4 0.3 fusion.52
  447.6 0.0 collective-permute-done.2
  447.7 2.7 collective-permute-done.3
  450.4 0.1 maximum_convert_fusion.1
  450.6 200.3 %all-gather.8.cloned.1.call-done = bf16[512,1024]{0,1:T(8,128)(2,1)} async-done(((bf16[512,8]{0,1:T(8,128)(2,1)}), bf16[512,1024]{0,1:T(8,128)(2,1)}) %all-gather.8.cloned.1.call-update) | async-done | bytes 1048592 | tf_op jit(solution)/shard_map/all_gather | solution.py:65
  650.8 4.8 convolution_convert_fusion.1
  655.6 0.0 all-reduce.2.cloned.1.call-update
  655.6 2.5 stack.2
  658.1 10.7 %all-to-all-start = ((bf16[128,8,2048]{2,1,0:T(8,128)(2,1)}), bf16[128,8,2048]{2,1,0:T(8,128)(2,1)}, u32[]{:S(2)}, u32[]{:S(2)}) async-start(bf16[128,8,2048]{2,1,0:T(8,128)(2,1)} %stack.2), calls=%async_computation | async-start | bytes 8388608 | tf_op jit(solution)/shard_map/all_to_all | solution.py:77
  668.8 0.0 all-gather.10.cloned.1.call-start
  668.8 0.5 all-gather.10.cloned.1.call-update
  669.4 0.2 reduce-scatter.2.cloned.1.call-start
  669.6 68.7 %all-reduce.2.cloned.1.call-done = bf16[512,1024]{1,0:T(8,128)(2,1)} async-done(((bf16[512,1024]{1,0:T(8,128)(2,1)}), bf16[512,1024]{1,0:T(8,128)(2,1)}) %all-reduce.2.cloned.1.call-update) | async-done | bytes 1048592 | tf_op jit(solution)/shard_map/psum | solution.py:70
  738.3 1.7 convert_add_fusion
  740.0 0.5 multiply_reduce_fusion
  740.5 22.3 %all-to-all-done = bf16[128,8,2048]{2,1,0:T(8,128)(2,1)} async-done(((bf16[128,8,2048]{2,1,0:T(8,128)(2,1)}), bf16[128,8,2048]{2,1,0:T(8,128)(2,1)}, u32[]{:S(2)}, u32[]{:S(2)}) %all-to-all-start) | async-done | bytes 4194336 | tf_op jit(solution)/shard_map/all_to_all | solution.py:77
  762.8 193.2 %all-gather.10.cloned.1.call-done = bf16[2048,1024]{0,1:T(8,128)(2,1)} async-done(((bf16[2048,8]{0,1:T(8,128)(2,1)}), bf16[2048,1024]{0,1:T(8,128)(2,1)}) %all-gather.10.cloned.1.call-update) | async-done | bytes 4194320 | tf_op jit(solution)/shard_map/all_gather | solution.py:84
  956.0 9.6 fusion.11
  965.7 0.0 reduce-scatter.2.cloned.1.call-update
  965.7 27.4 %reduce-scatter.2.cloned.1.call-done = bf16[256,1024]{1,0:T(8,128)(2,1)} async-done(((bf16[512,1024]{1,0:T(8,128)(2,1)}), bf16[256,1024]{1,0:T(8,128)(2,1)}) %reduce-scatter.2.cloned.1.call-update) | async-done | bytes 524304 | tf_op jit(solution)/shard_map/reduce_scatter | solution.py:87
  993.1 2.0 add_convert_fusion
  (9 shorter events, 0.0 us)
Async XLA Ops:
  6.5 218.8 %all-gather.12.cloned.1.call-start = ((), (), s32[]{:S(2)}) async-start(), calls=%async_computation.7 | async-start | bytes 2113536 | tf_op jit(solution)/shard_map/all_gather | solution.py:44
  7.3 432.5 %all-gather.6.cloned.1.call-start = ((), (), s32[]{:S(2)}) async-start(), calls=%async_computation.2 | async-start | bytes 2113536 | tf_op jit(solution)/shard_map/all_gather | solution.py:51
  8.7 642.2 %all-gather.8.cloned.1.call-start = ((), (), s32[]{:S(2)}) async-start(), calls=%async_computation.3 | async-start | bytes 1056768 | tf_op jit(solution)/shard_map/all_gather | solution.py:65
  9.4 10.1 %collective-permute-start = (bf16[7,768]{1,0:T(8,128)(2,1)S(1)}, bf16[7,768]{1,0:T(8,128)(2,1)S(1)}, u32[]{:S(2)}, u32[]{:S(2)}) collective-permute-start(bf16[7,768]{1,0:T(8,128)(2,1)S(1)} %get-tuple-element.22), channel_id=1, source_target_pairs={{0,1},{1,2},{2,3},{3,4},{4,5},{5,6},{6,7},{7,8},{8,9},{9,10},{10,1... | collective-permute-start | bytes 32264 | tf_op jit(solution)/shard_map/ppermute | solution.py:14
  15.1 5.9 collective-permute-start.1
  17.6 720.7 %all-reduce.2.cloned.1.call-start = ((), (), s32[]{:S(2)}) async-start(), calls=%async_computation.4 | async-start | bytes 2097152 | tf_op jit(solution)/shard_map/psum | solution.py:70
  443.0 4.7 collective-permute-start.2
  445.4 5.0 collective-permute-start.3
  650.8 4.8 copy-start.1
  658.1 104.7 %all-to-all-start = ((bf16[128,8,2048]{2,1,0:T(8,128)(2,1)}), bf16[128,8,2048]{2,1,0:T(8,128)(2,1)}, u32[]{:S(2)}, u32[]{:S(2)}) async-start(bf16[128,8,2048]{2,1,0:T(8,128)(2,1)} %stack.2), calls=%async_computation | async-start | bytes 8388608 | tf_op jit(solution)/shard_map/all_to_all | solution.py:77
  668.8 287.2 %all-gather.10.cloned.1.call-start = ((), (), s32[]{:S(2)}) async-start(), calls=%async_computation.5 | async-start | bytes 4227072 | tf_op jit(solution)/shard_map/all_gather | solution.py:84
  669.4 323.7 %reduce-scatter.2.cloned.1.call-start = ((), (), s32[]{:S(2)}) async-start(), calls=%async_computation.6 | async-start | bytes 1572864 | tf_op jit(solution)/shard_map/reduce_scatter | solution.py:87
  738.3 1.7 copy-start
Sparse Core Ops, SparseCore 0:
  9.2 216.0 all-gather.11
  227.2 212.4 all-gather.5
  441.6 209.1 all-gather.7
  655.7 82.5 all-reduce.1
  740.2 215.7 all-gather.9
  965.8 27.2 reduce-scatter.1
